TPU v7x, 32 devices: a whole 2x2x4 slice. The times are simulated.
32 devices in a mesh: bead: 8 (over z, x), space: 4 (over y, core).
Axes of the slice: x: 2, y: 2, z: 4, core: 2. Of those that a mesh axis runs over, the one named last changes fastest.
Arguments:
- positions: float32 [32, 64, 3, 128], P('bead', 'space'), may hold values from 0 to 1
- momenta: float32 [32, 64, 3, 128], P('bead', 'space'), may hold values from -3 to 3
- noise: float32 [32, 64, 3, 128], P('bead', 'space'), may hold values from -6 to 6
- atom_types: int32 [64, 128], P('space'), may hold values from 0 to 3
- occupancy: int32 [64], P('space'), may hold values from 64 to 128, as said below
- type_sigma: float32 [4], replicated, may hold values from 0.2 to 0.4
- type_eps: float32 [4], replicated, may hold values from 0.5 to 2
- type_mass: float32 [4], replicated, may hold values from 1 to 4
Outputs:
- new_positions: float32 [32, 64, 3, 128], P('bead', 'space')
- new_momenta: float32 [32, 64, 3, 128], P('bead', 'space')
Inputs may be any that keep to these rules, and one draw needn't show every extreme that they name: `occupancy`: in each domain of 16 consecutive cells some cell holds 128 atoms.
All inputs are finite; a program needn't handle non-finite values.
Results may differ from a plain program's by a relative error of at most 0.0002.
Values sent between devices are 32-bit elements; how exact they have to be, the bound alone decides.
No kernel may reach another device: no remote copies, remote signals or barrier semaphores. Data moves between devices by JAX's collectives and lax.ppermute only.
A program may use at most 64 MiB of HBM per device.

v0:
```python
import functools

import jax
import jax.numpy as jnp
import numpy as np
from jax import lax
from jax.experimental import pallas as pl
from jax.experimental.pallas import tpu as pltpu
from jax.sharding import PartitionSpec as P

PC = 8
GY = 4
GZ = 4

TIME_STEP = 0.05
INVERSE_TEMP = 32.0
CENTROID_FRICTION = 1.0
INNER_CUT = 0.5
OUTER_CUT = 1.0
CUBE_ROOT_TWO = 2.0 ** (1.0 / 3.0)
F32 = jnp.float32
BF16 = jnp.bfloat16
SPAN = 32
GROUP = 4
STEPS = ((SPAN // 2, 4), (SPAN // 2, 2), (SPAN // 2, 1), (SPAN, 2), (SPAN, 1))
VMEM_LIMIT = 48 * 1024 * 1024


def mode_matrix(number):
    rows = np.arange(number, dtype=np.float64)[:, None]
    column = np.arange(number, dtype=np.float64)[None, :]
    phases = 2.0 * np.pi * rows * column / number
    factor = np.sqrt(2.0 / number)
    middle = np.cos(np.pi * rows) / np.sqrt(number)
    matrix = np.where(column < number / 2, factor * np.cos(phases), factor * np.sin(phases))
    matrix = np.where(column == number / 2, middle, matrix)
    return np.where(column == 0, 1.0 / np.sqrt(number), matrix)


def contract_matrix(full_count, reduced):
    selected = np.arange(reduced)
    selected = np.where(selected <= reduced // 2, selected, selected + full_count - reduced)
    chosen = mode_matrix(full_count)[:, selected]
    return np.sqrt(reduced / full_count) * (mode_matrix(reduced) @ chosen.T)


def step_matrices(number):
    index = np.arange(number, dtype=np.float64)
    frequency = 2.0 * (number / INVERSE_TEMP) * np.sin(np.pi * index / number)
    friction = np.where(index == 0, CENTROID_FRICTION, 2.0 * frequency)
    damping = np.exp(-friction * TIME_STEP)
    kicking = np.sqrt((1.0 - damping * damping) / INVERSE_TEMP)
    cosine = np.cos(frequency * TIME_STEP)
    sine = np.sin(frequency * TIME_STEP)
    drift = np.where(index == 0, TIME_STEP, sine / np.where(index == 0, 1.0, frequency))
    modes = mode_matrix(number)

    def over_beads(diagonal):
        return (modes * diagonal[None, :]) @ modes.T

    return np.array(
        [
            [over_beads(cosine), over_beads(drift * damping), over_beads(drift * kicking)],
            [
                over_beads(-frequency * sine),
                over_beads(cosine * damping),
                over_beads(cosine * kicking),
            ],
        ]
    )


def partner_lists(domain_cells):
    lists = []
    for one in range(domain_cells):
        near = []
        for two in range(domain_cells):
            step_y, step_z = two // GZ - one // GZ, two % GZ - one % GZ
            if abs(step_y) <= 1 and abs(step_z) <= 1:
                near.append((two, step_y, step_z))
        later = [entry for entry in near if entry[0] > one]
        lists.append(later + [(two + domain_cells, y, z) for two, y, z in near])
    starts = np.cumsum([0] + [len(entries) for entries in lists]).astype(np.int32)
    return starts, np.array([value for entries in lists for entry in entries for value in entry], np.int32)


def pair_weight(h, radius_sq, terms, longer):
    inverse = pl.reciprocal(h, approx=True)
    if longer:
        quotient = terms[1] * inverse
        twice = quotient * quotient * quotient
        outer = jnp.maximum(1.0 - radius_sq, 0.0)
        inner = jnp.maximum(1.0 - 4.0 * radius_sq, 0.0)
        switch = outer * outer - inner * inner
        slope = outer - 4.0 * inner
        return twice * ((twice - 1.0) * (3.0 * (switch * inverse) + slope) - slope)
    quotient = terms[1] * inverse
    twice = quotient * quotient * quotient
    edge = jnp.maximum(terms[2] * inverse - 1.0, 2.0)
    bracket = edge * (twice - 1.0) - twice
    return (twice * bracket) * ((edge - 2.0) * h)


def weight_factor(longer):
    return 4.0 if longer else 64.0 / 3.0


def columns(block):
    few, lanes = block.shape
    return jnp.concatenate([block, jnp.zeros((8 - few, lanes), F32)], axis=0).T


def spread_rows(position, params, cell, rows_ref, size_ref):
    beads, lanes = position.shape[0], position.shape[-1]
    sizes = columns(params[cell, 0:2, :])
    for kind in range(2):
        size_ref[cell, kind] = jnp.broadcast_to(sizes[:, kind : kind + 1], (lanes, lanes))
    for bead in range(beads):
        block = columns(position[bead, cell])
        for axis in range(3):
            rows_ref[cell, bead, axis] = jnp.broadcast_to(
                block[:, axis : axis + 1], (lanes, lanes)
            )


def meet(longer, cell, first, partners, refs):
    lanes_ref, sizes_ref, rows_ref, size_ref, total_ref, back_ref = refs
    beads, lanes = lanes_ref.shape[0], lanes_ref.shape[-1]
    here = pl.ds(first, SPAN)
    row_half, row_root = size_ref[cell, 0, here, :], size_ref[cell, 1, here, :]
    known = []
    for partner, _, _ in partners:
        half = row_half + sizes_ref[partner, 0:1, :]
        s2 = half * half
        terms = (s2, CUBE_ROOT_TWO * s2, None if longer else 0.75 + 3.0 * s2)
        known.append((s2, terms, row_root * sizes_ref[partner, 1:2, :]))
    for bead in range(beads):
        rows = [rows_ref[cell, bead, axis, here, :] for axis in range(3)]
        back = [None, None, None]
        for (partner, step_y, step_z), (s2, terms, depth) in zip(partners, known):
            place = lanes_ref[bead, partner]
            apart = [
                place[0:1] - rows[0], (place[1:2] + step_y) - rows[1], (place[2:3] + step_z) - rows[2]
            ]
            radius_sq = apart[0] * apart[0] + apart[1] * apart[1] + apart[2] * apart[2]
            weight = depth * pair_weight(radius_sq + s2, radius_sq, terms, longer)
            for axis in range(3):
                push = weight * apart[axis]
                back[axis] = push if back[axis] is None else back[axis] + push
                if total_ref is not None:
                    total_ref[partner, bead, axis] += jnp.sum(
                        push.reshape(SPAN // 8, 8, lanes), axis=0
                    )
        for axis in range(3):
            if total_ref is None:
                back_ref[cell, bead, axis, here, :] = back[axis]
            else:
                back_ref[cell, bead, axis, here, :] += back[axis]


def fold_back(back_ref, cell, bead):
    lanes = back_ref.shape[-1]
    column = lax.broadcasted_iota(jnp.int32, (lanes, 8), 1)
    sums = [jnp.sum(back_ref[cell, bead, axis], axis=1, keepdims=True) for axis in range(3)]
    block = jnp.where(
        column == 0, sums[0], jnp.where(column == 1, sums[1], jnp.where(column == 2, sums[2], 0.0))
    )
    return block.T[0:3]


def fold_total(total_ref, cell, bead):
    return jnp.concatenate(
        [jnp.sum(total_ref[cell, bead, axis], axis=0, keepdims=True) for axis in range(3)], axis=0
    )


def pairs_kernel(
    longer, parts, plan, occupied, position, params, next_position, next_params,
    force_ref, other_ref, lanes_ref, sizes_ref, rows_ref, size_ref, total_ref, back_ref,
):
    beads, cells, _, lanes = position.shape
    factor = weight_factor(longer)
    together = max(1, 4 // beads)
    axis_row = lax.broadcasted_iota(jnp.int32, (3, lanes), 0)
    layer = jnp.where(axis_row == 0, 1.0, 0.0)
    for bead in range(beads):
        lanes_ref[bead, 0:cells] = position[bead]
        lanes_ref[bead, cells : 2 * cells] = next_position[bead] + layer[None]
    sizes_ref[0:cells] = params[:, 0:2, :]
    sizes_ref[cells : 2 * cells] = next_params[:, 0:2, :]
    total_ref[...] = jnp.zeros_like(total_ref)

    def spread(index, carry):
        for shift in range(together):
            spread_rows(position, params, index * together + shift, rows_ref, size_ref)
        return carry

    lax.fori_loop(0, cells // together, spread, 0)
    refs = (lanes_ref, sizes_ref, rows_ref, size_ref)

    def entry_of(entry):
        return (
            plan[cells + 1 + 3 * entry],
            plan[cells + 2 + 3 * entry].astype(F32),
            plan[cells + 3 + 3 * entry].astype(F32),
        )

    def per_cell(cell, carry):
        begin, end = plan[cell], plan[cell + 1]
        odd = lax.rem(end - begin, 2)

        def per_span(index, carry):
            firsts = [
                pl.multiple_of((index * parts + part) * SPAN, SPAN) for part in range(parts)
            ]
            for first in firsts:
                meet(longer, cell, first, [(cell, 0.0, 0.0)], refs + (None, back_ref))

            def single(entry, carry):
                for first in firsts:
                    meet(longer, cell, first, [entry_of(entry)], refs + (total_ref, back_ref))
                return carry

            def double(step, carry):
                entry = begin + odd + 2 * step
                both = [entry_of(entry), entry_of(entry + 1)]
                for first in firsts:
                    meet(longer, cell, first, both, refs + (total_ref, back_ref))
                return carry

            carry = lax.fori_loop(begin, begin + odd, single, carry)
            return lax.fori_loop(0, lax.div(end - begin, 2), double, carry)

        span = SPAN * parts
        return lax.fori_loop(0, lax.div(occupied[cell] + (span - 1), span), per_span, carry)

    lax.fori_loop(0, cells, per_cell, 0)

    def finish(index, carry):
        for shift in range(together):
            cell = index * together + shift
            alive = params[cell, 1:2, :] > 0.0
            for bead in range(beads):
                total = fold_total(total_ref, cell, bead) - fold_back(back_ref, cell, bead)
                force_ref[bead, cell] = jnp.where(alive, factor * total, 0.0)
                other_ref[bead, cell] = factor * fold_total(total_ref, cell + cells, bead)
        return carry

    lax.fori_loop(0, cells // together, finish, 0)


def octant_key(x, y, z, alive):
    zed = jnp.where(z >= 0.5, 1.0, 0.0)
    gray = jnp.where(y >= 0.5, 3.0 - zed, zed)
    return jnp.where(alive, jnp.where(x >= 0.5, 7.0 - gray, gray), 8.0)


def reach_lists(domain_cells):
    octants = []
    for bit_x in range(2):
        for bit_y in range(2):
            for bit_z in range(2):
                gray = 3 - bit_z if bit_y else bit_z
                octants.append((7 - gray if bit_x else gray, (bit_x, bit_y, bit_z)))
    classes = [[[] for _ in range(domain_cells)] for _ in STEPS]
    for one in range(domain_cells):
        runs = {}
        for layer in range(2):
            for two in range(domain_cells):
                step = (layer, two // GZ - one // GZ, two % GZ - one % GZ)
                if abs(step[1]) > 1 or abs(step[2]) > 1 or (layer == 0 and two <= one):
                    continue
                keys = [
                    key
                    for key, bits in octants
                    if all(move == 0 or bit == (move > 0) for move, bit in zip(step, bits))
                ]
                entry = (two + layer * domain_cells, step[1], step[2], min(keys), max(keys) + 1)
                runs.setdefault(entry[4] - entry[3], []).append(entry)
        for length, entries in sorted(runs.items()):
            entries.sort(key=lambda entry: entry[3:])
            span = SPAN // 2 if length == 1 else SPAN
            for place, (rows, count) in enumerate(STEPS):
                if rows == span:
                    whole = len(entries) // count * count
                    classes[place][one] += entries[:whole]
                    entries = entries[whole:]
    starts, values = [], []
    for lists in classes:
        for entries in lists:
            starts.append(len(values) // 5)
            values += [value for entry in entries for value in entry]
        starts.append(len(values) // 5)
    return np.array(starts, np.int32), np.array(values, np.int32)


def split_three(value):
    high = value.astype(BF16).astype(F32)
    rest = value - high
    middle = rest.astype(BF16).astype(F32)
    return high, middle, rest - middle


def order_kernel(position, params, out_ref):
    beads, cells, _, lanes = position.shape
    row = lax.broadcasted_iota(jnp.int32, (lanes, lanes), 0)
    column = lax.broadcasted_iota(jnp.int32, (lanes, lanes), 1)
    before = jnp.where(row < column, 1.0, 0.0).astype(BF16)
    counter = jnp.concatenate([before, jnp.ones((lanes, lanes), BF16)], axis=0)
    kind = lax.broadcasted_iota(jnp.int32, (16, lanes), 0).astype(F32)
    place_row = row.astype(F32)

    def per_cell(index, carry):
        for shift, bead in [(shift, bead) for shift in range(GROUP) for bead in range(beads)]:
            cell = index * GROUP + shift
            sizes = params[cell, 0:2, :]
            place = position[bead, cell]
            key = octant_key(place[0:1], place[1:2], place[2:3], sizes[1:2] > 0.0)
            same = jnp.where(key == kind, 1.0, 0.0)
            less = jnp.where(key < kind, 1.0, 0.0)
            counts = lax.dot_general(
                jnp.concatenate([same, less], axis=1).astype(BF16),
                counter,
                (((1,), (0,)), ((), ())),
                preferred_element_type=F32,
            )
            rank = jnp.sum(same * counts, axis=0, keepdims=True)
            chosen = jnp.where(rank == place_row, 1.0, 0.0).astype(BF16)
            block = jnp.concatenate([place, sizes, jnp.zeros((3, lanes), F32)], axis=0)
            moved = lax.dot_general(
                jnp.concatenate(split_three(block), axis=0).astype(BF16),
                chosen,
                (((1,), (1,)), ((), ())),
                preferred_element_type=F32,
            )
            out_ref[bead, cell, 0:5, :] = (moved[0:8] + moved[8:16] + moved[16:24])[0:5]
            out_ref[bead, cell, 5:6, :] = rank
            out_ref[bead, cell, 6:8, :] = jnp.zeros((2, lanes), F32)
        return carry

    lax.fori_loop(0, cells // GROUP, per_cell, 0)


def meet_runs(span, local, runs, lanes_ref, sizes_ref, rows_ref, total_ref, back_ref):
    beads, lanes = lanes_ref.shape[0], lanes_ref.shape[-1]
    for bead in range(beads):
        for firsts, partner, step_y, step_z in runs:
            here = pl.ds(firsts[bead], span)
            half = rows_ref[local, bead, 3, here, :] + sizes_ref[partner, 0:1, :]
            s2 = half * half
            terms = (s2, CUBE_ROOT_TWO * s2, 0.75 + 3.0 * s2)
            place = lanes_ref[bead, partner]
            apart = [
                place[0:1] - rows_ref[local, bead, 0, here, :],
                (place[1:2] + step_y) - rows_ref[local, bead, 1, here, :],
                (place[2:3] + step_z) - rows_ref[local, bead, 2, here, :],
            ]
            radius_sq = apart[0] * apart[0] + apart[1] * apart[1] + apart[2] * apart[2]
            depth = rows_ref[local, bead, 4, here, :] * sizes_ref[partner, 1:2, :]
            weight = depth * pair_weight(radius_sq + s2, radius_sq, terms, False)
            for axis in range(3):
                push = weight * apart[axis]
                if total_ref is None:
                    back_ref[local, bead, axis, here, :] = push
                else:
                    back_ref[local, bead, axis, here, :] += push
                    total_ref[partner, bead, axis] += jnp.sum(
                        push.reshape(span // 8, 8, lanes), axis=0
                    )


def reach_kernel(
    plan, position, params, next_position, next_params, ordered, force_ref, other_ref, lanes_ref,
    sizes_ref, rows_ref, total_ref, back_ref,
):
    beads, cells, _, lanes = position.shape
    entries_at = len(STEPS) * (cells + 1)
    bounds_at = plan.shape[0] - beads * cells * 9
    factor = weight_factor(False)
    axis_row = lax.broadcasted_iota(jnp.int32, (3, lanes), 0)
    layer = jnp.where(axis_row == 0, 1.0, 0.0)
    for bead in range(beads):
        lanes_ref[bead, 0:cells] = position[bead]
        lanes_ref[bead, cells : 2 * cells] = next_position[bead] + layer[None]
    sizes_ref[0:cells] = params[:, 0:2, :]
    sizes_ref[cells : 2 * cells] = next_params[:, 0:2, :]
    total_ref[...] = jnp.zeros_like(total_ref)
    rows_ref[:, :, :, lanes:, :] = jnp.zeros((GROUP, beads, 5, SPAN, lanes), F32)
    row = lax.broadcasted_iota(jnp.int32, (lanes, lanes), 0).astype(F32)
    slot = lax.broadcasted_iota(jnp.int32, (8, lanes), 1)
    column = lax.broadcasted_iota(jnp.int32, (lanes, 8), 1)
    refs = (lanes_ref, sizes_ref, rows_ref)
    every = [(local, bead) for local in range(GROUP) for bead in range(beads)]

    def per_group(group, carry):
        for local, bead in every:
            block = ordered[bead, group * GROUP + local].T
            for axis in range(5):
                rows_ref[local, bead, axis, 0:lanes, :] = jnp.broadcast_to(
                    block[:, axis : axis + 1], (lanes, lanes)
                )

        def per_cell(local, carry):
            cell = group * GROUP + local

            def bound(bead, octant):
                return plan[bounds_at + (bead * cells + cell) * 9 + octant]

            def itself(index, carry):
                first = pl.multiple_of(index * SPAN, SPAN)
                run = ([first] * beads, cell, 0.0, 0.0)
                meet_runs(SPAN, local, [run], *refs, None, back_ref)
                return carry

            lax.fori_loop(0, lax.div(bound(0, 8) + (SPAN - 1), SPAN), itself, 0)

            for place, (span, count) in enumerate(STEPS):
                begin = plan[place * (cells + 1) + cell]
                end = plan[place * (cells + 1) + cell + 1]

                def per_step(step, carry, span=span, count=count, begin=begin):
                    runs, longest = [], 0
                    for shift in range(count):
                        at = entries_at + 5 * (begin + step * count + shift)
                        begins = [bound(bead, plan[at + 3]) for bead in range(beads)]
                        for bead in range(beads):
                            longest = jnp.maximum(longest, bound(bead, plan[at + 4]) - begins[bead])
                        runs.append(
                            (begins, plan[at], plan[at + 1].astype(F32), plan[at + 2].astype(F32))
                        )

                    def per_span(index, carry):
                        moved = [
                            ([jnp.minimum(first + index * span, lanes) for first in begins], *rest)
                            for begins, *rest in runs
                        ]
                        meet_runs(span, local, moved, *refs, total_ref, back_ref)
                        return carry

                    return lax.fori_loop(0, lax.div(longest + (span - 1), span), per_span, carry)

                lax.fori_loop(0, lax.div(end - begin, count), per_step, 0)
            return carry

        lax.fori_loop(0, GROUP, per_cell, 0)

        for local, bead in every:
            cell = group * GROUP + local
            alive = plan[bounds_at + cell * 9 + 8]
            sums = [
                jnp.sum(back_ref[local, bead, axis, 0:lanes, :], axis=1, keepdims=True)
                for axis in range(3)
            ]
            block = jnp.where(
                column == 0,
                sums[0],
                jnp.where(column == 1, sums[1], jnp.where(column == 2, sums[2], 0.0)),
            ).T
            block = jnp.where(slot < alive, block, 0.0)
            chosen = jnp.where(ordered[bead, cell, 5:6, :] == row, 1.0, 0.0).astype(BF16)
            moved = lax.dot_general(
                jnp.concatenate(split_three(block), axis=0).astype(BF16),
                chosen,
                (((1,), (0,)), ((), ())),
                preferred_element_type=F32,
            )
            force_ref[bead, cell] = (moved[0:8] + moved[8:16] + moved[16:24])[0:3]
        return carry

    lax.fori_loop(0, cells // GROUP, per_group, 0)

    def finish(index, carry):
        for shift, bead in every:
            cell = index * GROUP + shift
            total = fold_total(total_ref, cell, bead) - force_ref[bead, cell]
            force_ref[bead, cell] = factor * total
            other_ref[bead, cell] = factor * fold_total(total_ref, cell + cells, bead)
        return carry

    lax.fori_loop(0, cells // GROUP, finish, 0)


def short_forces(position, params, next_position, next_params, ordered, bounds):
    beads, cells, _, lanes = position.shape
    starts, entries = reach_lists(cells)
    plan = jnp.concatenate([jnp.asarray(starts), jnp.asarray(entries), bounds])
    forces = jax.ShapeDtypeStruct((beads, cells, 3, lanes), F32)
    return call(
        reach_kernel,
        (plan, position, params, next_position, next_params, ordered),
        1,
        (forces, forces),
        [
            pltpu.VMEM((beads, 2 * cells, 3, lanes), F32),
            pltpu.VMEM((2 * cells, 2, lanes), F32),
            pltpu.VMEM((GROUP, beads, 5, lanes + SPAN, lanes), F32),
            pltpu.VMEM((2 * cells, beads, 3, 8, lanes), F32),
            pltpu.VMEM((GROUP, beads, 3, lanes + SPAN, lanes), F32),
        ],
        PAIR_FLOPS * beads * 70,
    )


def call(kernel, inputs, smem, outputs, scratch, flops):
    return pl.pallas_call(
        kernel,
        out_shape=outputs,
        in_specs=[
            pl.BlockSpec(memory_space=pltpu.SMEM if place < smem else pltpu.VMEM)
            for place in range(len(inputs))
        ],
        scratch_shapes=scratch,
        compiler_params=pltpu.CompilerParams(vmem_limit_bytes=VMEM_LIMIT),
        cost_estimate=pl.CostEstimate(flops=flops, bytes_accessed=1 << 18, transcendentals=0),
    )(*inputs)


PAIR_FLOPS = 40 * 128 * 128


def pair_forces(position, params, occupied, next_position, next_params, longer):
    beads, cells, _, lanes = position.shape
    starts, entries = partner_lists(cells)
    forces = jax.ShapeDtypeStruct((beads, cells, 3, lanes), F32)
    return call(
        functools.partial(pairs_kernel, longer, lanes // SPAN if longer else 1),
        (
            jnp.asarray(np.concatenate([starts, entries])), occupied, position, params,
            next_position, next_params,
        ),
        2,
        (forces, forces),
        [
            pltpu.VMEM((beads, 2 * cells, 3, lanes), F32),
            pltpu.VMEM((2 * cells, 2, lanes), F32),
            pltpu.VMEM((cells, beads, 3, lanes, lanes), F32),
            pltpu.VMEM((cells, 2, lanes, lanes), F32),
            pltpu.VMEM((2 * cells, beads, 3, 8, lanes), F32),
            pltpu.VMEM((cells, beads, 3, lanes, lanes), F32),
        ],
        PAIR_FLOPS * beads * (len(entries) // 3 + cells),
    )


def kick_kernel(
    piece_rows, groups, table, rank, position, momenta, noise, force, back, params, partial_ref, piece_ref
):
    beads, cells = position.shape[:2]
    holders = piece_ref.shape[0]
    reduced = table.shape[0]
    first = rank[0] * beads
    if holders * piece_rows > 3 * cells:
        piece_ref[...] = jnp.zeros_like(piece_ref)
    for cell in range(cells):
        mass = params[cell, 2:3, :]
        per_mass = 1.0 / mass
        per_root = lax.rsqrt(mass)
        per_root = per_root * (1.5 - 0.5 * mass * per_root * per_root)
        inputs = []
        for bead in range(beads):
            kicked = momenta[bead, cell] + 0.5 * TIME_STEP * (force[bead, cell] + back[bead, cell])
            inputs.append((position[bead, cell], kicked * per_mass, noise[bead, cell] * per_root))
        for bead in range(beads):
            for kind in range(3):
                base = (kind * beads + bead) * piece_rows
                if piece_rows % 3 == 0:
                    owner, row = divmod(3 * cell, piece_rows)
                    piece_ref[owner, base + row : base + row + 3, :] = inputs[bead][kind]
                else:
                    for axis in range(3):
                        owner, row = divmod(3 * cell + axis, piece_rows)
                        piece_ref[owner, base + row : base + row + 1, :] = inputs[bead][kind][
                            axis : axis + 1
                        ]
        for group in range(reduced):
            total = None
            for bead in range(beads):
                for kind in range(3):
                    term = table[group, kind * holders * beads + first + bead] * inputs[bead][kind]
                    total = term if total is None else total + term
            for copy in range(groups):
                partial_ref[group * groups + copy, 3 * cell : 3 * cell + 3, :] = total


def move_kernel(piece_rows, beads, matrix, arrived, out_ref, gathered):
    holders = arrived.shape[0]
    taken = 3 * beads
    given = 2 * beads
    for row in range(piece_rows):
        for holder in range(holders):
            gathered[row, holder * taken : (holder + 1) * taken, :] = arrived[
                holder, pl.ds(row, taken, stride=piece_rows), :
            ]
        moved = lax.dot_general(
            matrix[...],
            gathered[row],
            (((1,), (0,)), ((), ())),
            precision=lax.Precision.HIGHEST,
            preferred_element_type=F32,
        )
        for holder in range(holders):
            out_ref[holder, row * given : (row + 1) * given, :] = moved[
                holder * given : (holder + 1) * given
            ]


def finish_kernel(piece_rows, groups, table, rank, moved, slow, params, position_ref, momentum_ref):
    beads, cells = position_ref.shape[:2]
    given = 2 * beads
    reduced = table.shape[0]
    first = rank[0] * beads
    for cell in range(cells):
        mass = params[cell, 2:3, :]
        for bead in range(beads):
            def taken(kind):
                if piece_rows % 3 == 0:
                    owner, row = divmod(3 * cell, piece_rows)
                    return moved[owner, pl.ds(row * given + kind * beads + bead, 3, stride=given), :]
                rows = []
                for axis in range(3):
                    owner, row = divmod(3 * cell + axis, piece_rows)
                    place = row * given + kind * beads + bead
                    rows.append(moved[owner, place : place + 1, :])
                return jnp.concatenate(rows, axis=0)

            position_ref[bead, cell] = taken(0)
            total = mass * taken(1)
            for group in range(reduced):
                total = total + table[group, first + bead] * slow[
                    group * groups, 3 * cell : 3 * cell + 3, :
                ]
            momentum_ref[bead, cell] = total


def shards(positions, momenta, noise, atom_types, occupancy, type_sigma, type_eps, type_mass):
    beads, cells, _, lanes = positions.shape
    holders = lax.axis_size("bead")
    domains = lax.axis_size("space")
    rank = lax.axis_index("bead")
    total_beads = beads * holders
    rows = 3 * cells
    piece_rows = -(-rows // holders)
    held = max(1, PC // holders)
    groups = max(1, holders // PC)
    contract = contract_matrix(total_beads, PC)
    steps = step_matrices(total_beads)
    rank_table = rank.astype(jnp.int32).reshape(1)
    one_back = [((i + 1) % domains, i) for i in range(domains)]
    one_on = [(i, (i + 1) % domains) for i in range(domains)]

    codes = jnp.arange(type_sigma.shape[0])
    onehot = atom_types[..., None] == codes
    living = jnp.arange(lanes)[None, :] < occupancy[:, None]
    half_sigma = 0.5 * jnp.sum(jnp.where(onehot, type_sigma, 0.0), -1)
    root_eps = jnp.sqrt(jnp.sum(jnp.where(onehot, type_eps, 0.0), -1))
    mass = jnp.sum(jnp.where(onehot, type_mass, 0.0), -1)
    params = jnp.stack([half_sigma, jnp.where(living, root_eps, 0.0), mass], 1)

    stacked = jnp.concatenate([positions, params[None]], 0)
    next_stacked = lax.ppermute(stacked, "space", one_back)
    next_params = next_stacked[beads]
    ordered = call(
        order_kernel,
        (positions, params),
        0,
        jax.ShapeDtypeStruct((beads, cells, 8, lanes), F32),
        [],
        1 << 22,
    )
    key = octant_key(positions[:, :, 0], positions[:, :, 1], positions[:, :, 2], living[None])
    bounds = jnp.sum(
        (key[:, :, None, :] < jnp.arange(9, dtype=F32)[:, None]).astype(jnp.int32), -1
    )
    force, back = short_forces(
        positions, params, next_stacked[:beads], next_params, ordered, bounds.reshape(-1)
    )
    back = lax.ppermute(back, "space", one_on)

    position_map = np.concatenate([contract @ steps[0, kind] for kind in range(3)], axis=1)
    partial, pieces = call(
        functools.partial(kick_kernel, piece_rows, groups),
        (
            jnp.asarray(position_map, F32), rank_table, positions, momenta, noise, force, back,
            params,
        ),
        2,
        (
            jax.ShapeDtypeStruct((PC * groups, rows, lanes), F32),
            jax.ShapeDtypeStruct((holders, 3 * beads * piece_rows, lanes), F32),
        ),
        [],
        1 << 22,
    )
    arrived = lax.all_to_all(
        partial.reshape(holders, held * rows, lanes), "bead", split_axis=0, concat_axis=0, tiled=True
    )
    contracted = jnp.sum(arrived, 0).reshape(held, cells, 3, lanes)
    next_contracted = lax.ppermute(contracted, "space", one_back)
    pieces = lax.all_to_all(pieces, "bead", split_axis=0, concat_axis=0, tiled=True)
    slow, slow_back = pair_forces(
        contracted, params, occupancy, next_contracted, next_params, True
    )
    slow = slow + lax.ppermute(slow_back, "space", one_on)

    order = steps.reshape(2, 3, holders, beads, holders, beads).transpose(2, 0, 3, 4, 1, 5)
    order = order.reshape(2 * total_beads, 3 * total_beads)
    moved = call(
        functools.partial(move_kernel, piece_rows, beads),
        (jnp.asarray(order, F32), pieces),
        0,
        jax.ShapeDtypeStruct((holders, 2 * beads * piece_rows, lanes), F32),
        [pltpu.VMEM((piece_rows, 3 * total_beads, lanes), F32)],
        1 << 23,
    )
    moved_rows = 2 * beads * piece_rows
    sent = jnp.concatenate(
        [
            moved,
            jnp.broadcast_to(slow.reshape(1, held * rows, lanes), (holders, held * rows, lanes)),
        ],
        1,
    )
    got = lax.all_to_all(sent, "bead", split_axis=0, concat_axis=0, tiled=True)
    spread = 0.5 * TIME_STEP * (total_beads / PC) * contract
    shape = jax.ShapeDtypeStruct(positions.shape, F32)
    return call(
        functools.partial(finish_kernel, piece_rows, groups),
        (
            jnp.asarray(spread, F32), rank_table, got[:, :moved_rows],
            got[:, moved_rows:].reshape(holders * held, rows, lanes), params,
        ),
        2,
        (shape, shape),
        [],
        1 << 20,
    )


def solution(mesh):
    placed = (
        P("bead", "space", None, None),
        P("bead", "space", None, None),
        P("bead", "space", None, None),
        P("space", None),
        P("space"),
        P(),
        P(),
        P(),
    )
    return jax.shard_map(
        shards,
        mesh=mesh,
        in_specs=placed,
        out_specs=(P("bead", "space", None, None), P("bead", "space", None, None)),
        check_vma=False,
    )
```

profile of v0, /device:TPU:0, one launch (start us, length us, event | category | flops | bytes accessed | tf_op | source)
XLA Modules:
  0.0 134.2 jit_solution(6341693375061576686)
XLA Ops:
  0.6 0.8 select_reduce_fusion.2
  1.4 0.9 copy.36.position
  2.4 0.0 copy-start.3
  2.4 0.6 copy-done.3
  3.1 0.1 compare_select_fusion
  3.2 0.0 copy-start.5
  3.2 2.5 %collective-permute-start = (f32[5,16,3,128]{3,2,1,0:T(4,128)S(1)}, f32[5,16,3,128]{3,2,1,0:T(4,128)S(1)}, u32[]{:S(2)}, u32[]{:S(2)}) collective-permute-start(f32[5,16,3,128]{3,2,1,0:T(4,128)S(1)} %pad_maximum_fusion.1), channel_id=1, source_target_pairs={{1,0},{2,1},{3,2},{0,3},{5,4},{6,5},{7,6},{4,7},{9,8},{10,9},{11,1... | collective-permute-start | bytes 368648 | tf_op jit(solution)/shard_map/ppermute | solution.py:660
  5.7 0.1 iota_compare_fusion.2
  5.8 0.0 copy-done.5
  5.8 0.7 convert_reduce_fusion
  6.5 0.1 copy.32
  6.6 0.0 copy-start.8
  6.6 0.0 copy-start.9
  6.6 0.1 reshape.80
  6.7 0.5 copy-done.8
  7.3 0.0 copy-done.9
  7.3 0.1 concatenate.9.plan
  7.4 6.1 %shard_map.149.ordered = f32[4,16,8,128]{3,2,1,0:T(8,128)S(1)} custom-call(f32[4,16,3,128]{3,2,1,0:T(4,128)S(1)} %copy.36.position, f32[16,3,128]{2,1,0:T(4,128)S(1)} %get-tuple-element.26.params), custom_call_target="tpu_custom_call" | custom-call | flops 4194304 | bytes 262144 | tf_op jit(solution)/shard_map/pallas_call | solution.py:505
  13.5 0.0 collective-permute-done
  13.5 0.0 copy-start.6
  13.5 44.3 %shard_map.150 = (f32[4,16,3,128]{3,2,1,0:T(4,128)S(1)}, f32[4,16,3,128]{3,2,1,0:T(4,128)S(1)}) custom-call(s32[1371]{0:T(1024)S(1)} %concatenate.9.plan, f32[4,16,3,128]{3,2,1,0:T(4,128)S(1)} %copy.36.position, f32[16,3,128]{2,1,0:T(4,128)S(1)} %get-tuple-element.26.params, f32[4,16,3,128]{3,2,1,0:T(4,128)S(1)} %slice.28.next_position, ...), custom_call_target="tpu_custom_call" | custom-call | flops 183500800 | bytes 262144 | tf_op jit(solution)/shard_map/pallas_call | solution.py:505
  57.8 3.4 %collective-permute-start.1 = (f32[4,16,3,128]{3,2,1,0:T(4,128)S(1)}, f32[4,16,3,128]{3,2,1,0:T(4,128)S(1)}, u32[]{:S(2)}, u32[]{:S(2)}) collective-permute-start(f32[4,16,3,128]{3,2,1,0:T(4,128)S(1)} %get-tuple-element.9), channel_id=1, source_target_pairs={{0,1},{1,2},{2,3},{3,0},{4,5},{5,6},{6,7},{7,4},{8,9},{9,10},{10,1... | collective-permute-start | bytes 294920 | tf_op jit(solution)/shard_map/ppermute | solution.py:677
  61.3 0.0 copy-done.6
  61.3 0.0 copy-start.7
  61.3 0.1 copy.37.momenta
  61.3 0.8 copy-done.7
  62.2 0.0 copy-start.2
  62.2 0.1 copy.38.noise
  62.2 0.9 collective-permute-done.1.back
  63.1 0.0 copy-done.2
  63.1 2.6 %shard_map.151 = (f32[8,48,128]{2,1,0:T(8,128)S(1)}, f32[8,72,128]{2,1,0:T(8,128)}) custom-call(f32[8,96]{1,0:T(8,128)S(1)} %copy-done.2, s32[1]{0:T(128)} %bitcast.rank, f32[4,16,3,128]{3,2,1,0:T(4,128)S(1)} %copy.36.position, f32[4,16,3,128]{3,2,1,0:T(4,128)S(1)} %copy.37.momenta, f32[4,16,3,128]{3,2,1,0:T(4,128)S(1)} %copy.38.noise, ...), custom_call_target="tpu_custom_call" | custom-call | flops 4194304 | bytes 262144 | tf_op jit(solution)/shard_map/pallas_call | solution.py:505
  65.6 16.6 %all_to_all.15 = f32[8,48,128]{2,1,0:T(8,128)S(1)} all-to-all(f32[8,48,128]{2,1,0:T(8,128)S(1)} %get-tuple-element.11), channel_id=1, replica_groups=mesh['bead'=8,'space'=4] {'bead'}, dimensions={0} | all-to-all | bytes 393216 | tf_op jit(solution)/shard_map/all_to_all | solution.py:694
  82.3 3.4 %all-to-all-start = ((f32[8,72,128]{2,1,0:T(8,128)}), f32[8,72,128]{2,1,0:T(8,128)S(1)}, u32[]{:S(2)}, u32[]{:S(2)}) async-start(f32[8,72,128]{2,1,0:T(8,128)} %get-tuple-element.10), calls=%async_computation | async-start | bytes 589824 | tf_op jit(solution)/shard_map/all_to_all | solution.py:699
  85.7 0.0 copy-start.4
  85.8 0.1 collective-permute-start.2
  85.8 1.6 %collective-permute-done.2.next_position = f32[1,16,3,128]{3,2,1,0:T(4,128)S(1)} collective-permute-done((f32[1,16,3,128]{3,2,1,0:T(4,128)S(1)}, f32[1,16,3,128]{3,2,1,0:T(4,128)S(1)}, u32[]{:S(2)}, u32[]{:S(2)}) %collective-permute-start.2) | collective-permute-done | bytes 24608 | tf_op jit(solution)/shard_map/ppermute | solution.py:698
  87.4 0.0 copy-done.4
  87.4 21.1 %shard_map.153 = (f32[1,16,3,128]{3,2,1,0:T(4,128)S(1)}, f32[1,16,3,128]{3,2,1,0:T(4,128)S(1)}) custom-call(s32[443]{0:T(512)S(1)} %copy-done.4, s32[16]{0:T(128)S(1)} %copy-done.3, f32[1,16,3,128]{3,2,1,0:T(4,128)S(1)} %reshape.81.position, f32[16,3,128]{2,1,0:T(4,128)S(1)} %get-tuple-element.26.params, ...), custom_call_target="tpu_custom_call" | custom-call | flops 103546880 | bytes 262144 | tf_op jit(solution)/shard_map/pallas_call | solution.py:505
  108.5 2.4 %collective-permute-start.3 = (f32[1,16,3,128]{3,2,1,0:T(4,128)S(1)}, f32[1,16,3,128]{3,2,1,0:T(4,128)S(1)}, u32[]{:S(2)}, u32[]{:S(2)}) collective-permute-start(f32[1,16,3,128]{3,2,1,0:T(4,128)S(1)} %get-tuple-element.13), channel_id=1, source_target_pairs={{0,1},{1,2},{2,3},{3,0},{4,5},{5,6},{6,7},{7,4},{8,9},{9,10},{10,1... | collective-permute-start | bytes 73736 | tf_op jit(solution)/shard_map/ppermute | solution.py:703
  110.9 0.9 collective-permute-done.3
  111.9 0.0 copy-start
  111.9 0.0 all-to-all-done.arrived
  111.9 0.7 copy-done
  112.6 0.4 shard_map.152
  113.1 18.1 %all_to_all.16 = f32[8,96,128]{2,1,0:T(8,128)S(1)} all-to-all(f32[8,96,128]{2,1,0:T(8,128)S(1)} %pad_maximum_fusion), channel_id=1, replica_groups=mesh['bead'=8,'space'=4] {'bead'}, dimensions={0} | all-to-all | bytes 786432 | tf_op jit(solution)/shard_map/all_to_all | solution.py:723
  131.2 0.0 copy-start.1
  131.2 0.7 copy-done.1
  131.9 1.0 shard_map.154
  132.9 0.6 copy.39
  133.5 0.6 copy.40
  (14 shorter events, 0.3 us)
Async XLA Ops:
  2.4 0.7 copy-start.3
  3.2 2.6 %copy-start.5 = (f32[4,16,3,128]{3,1,2,0:T(8,128)S(1)}, f32[4,16,3,128]{3,1,2,0:T(8,128)}, u32[]{:S(2)}) copy-start(f32[4,16,3,128]{3,1,2,0:T(8,128)} %param.14) | copy-start | bytes 294916
  3.2 10.2 %collective-permute-start = (f32[5,16,3,128]{3,2,1,0:T(4,128)S(1)}, f32[5,16,3,128]{3,2,1,0:T(4,128)S(1)}, u32[]{:S(2)}, u32[]{:S(2)}) collective-permute-start(f32[5,16,3,128]{3,2,1,0:T(4,128)S(1)} %pad_maximum_fusion.1), channel_id=1, source_target_pairs={{1,0},{2,1},{3,2},{0,3},{5,4},{6,5},{7,6},{4,7},{9,8},{10,9},{11,1... | collective-permute-start | bytes 368648 | tf_op jit(solution)/shard_map/ppermute | solution.py:660
  6.6 0.7 copy-start.8
  6.6 0.7 copy-start.9
  13.5 47.7 %copy-start.6 = (f32[4,16,3,128]{3,1,2,0:T(8,128)S(1)}, f32[4,16,3,128]{3,1,2,0:T(8,128)}, u32[]{:S(2)}) copy-start(f32[4,16,3,128]{3,1,2,0:T(8,128)} %param.15) | copy-start | bytes 294916
  57.8 5.3 %collective-permute-start.1 = (f32[4,16,3,128]{3,2,1,0:T(4,128)S(1)}, f32[4,16,3,128]{3,2,1,0:T(4,128)S(1)}, u32[]{:S(2)}, u32[]{:S(2)}) collective-permute-start(f32[4,16,3,128]{3,2,1,0:T(4,128)S(1)} %get-tuple-element.9), channel_id=1, source_target_pairs={{0,1},{1,2},{2,3},{3,0},{4,5},{5,6},{6,7},{7,4},{8,9},{9,10},{10,1... | collective-permute-start | bytes 294920 | tf_op jit(solution)/shard_map/ppermute | solution.py:677
  61.3 0.9 copy-start.7
  62.2 0.9 copy-start.2
  82.3 29.6 %all-to-all-start = ((f32[8,72,128]{2,1,0:T(8,128)}), f32[8,72,128]{2,1,0:T(8,128)S(1)}, u32[]{:S(2)}, u32[]{:S(2)}) async-start(f32[8,72,128]{2,1,0:T(8,128)} %get-tuple-element.10), calls=%async_computation | async-start | bytes 589824 | tf_op jit(solution)/shard_map/all_to_all | solution.py:699
  85.7 1.7 %copy-start.4 = (s32[443]{0:T(512)S(1)}, s32[443]{0:T(512)}, u32[]{:S(2)}) copy-start(s32[443]{0:T(512)} %constant.36.clone.plan) | copy-start | bytes 5320
  85.8 1.7 %collective-permute-start.2 = (f32[1,16,3,128]{3,2,1,0:T(4,128)S(1)}, f32[1,16,3,128]{3,2,1,0:T(4,128)S(1)}, u32[]{:S(2)}, u32[]{:S(2)}) collective-permute-start(f32[1,16,3,128]{3,2,1,0:T(4,128)S(1)} %reshape.81.position), channel_id=1, source_target_pairs={{1,0},{2,1},{3,2},{0,3},{5,4},{6,5},{7,6},{4,7},{9,8},{10,9},{11,1... | collective-permute-start | bytes 73736 | tf_op jit(solution)/shard_map/ppermute | solution.py:698
  108.5 3.4 %collective-permute-start.3 = (f32[1,16,3,128]{3,2,1,0:T(4,128)S(1)}, f32[1,16,3,128]{3,2,1,0:T(4,128)S(1)}, u32[]{:S(2)}, u32[]{:S(2)}) collective-permute-start(f32[1,16,3,128]{3,2,1,0:T(4,128)S(1)} %get-tuple-element.13), channel_id=1, source_target_pairs={{0,1},{1,2},{2,3},{3,0},{4,5},{5,6},{6,7},{7,4},{8,9},{9,10},{10,1... | collective-permute-start | bytes 73736 | tf_op jit(solution)/shard_map/ppermute | solution.py:703
  111.9 0.8 copy-start
  131.2 0.7 copy-start.1
where the time goes:
time: 132 us; the launch traced here: 134 us
  Pallas kernels  75.4 us (57%)
  blocking collectives  34.8 us (26%)
  starting transfers between devices  11.8 us (9%)
  local copies, waits for them, and re-layouts  6.23 us (5%)
  waiting for transfers between devices  3.39 us (3%)
  other arithmetic  1.76 us (1%)
    pallas_call x6, Pallas kernels, call(): pl.pallas_call(kernel, out_shape=outputs, in_specs=[pl.BlockSpec(memory_s...  75.4 us
    all_to_all x1, blocking collectives, shards(): got = lax.all_to_all(sent, 'bead', split_axis=0, concat_axis=0, tiled=True)  18.1 us
    all_to_all x1, blocking collectives, shards(): lax.all_to_all(partial.reshape(holders, held * rows, lanes), 'bead', spli...  16.6 us
    unnamed x23, local copies, waits for them, and re-layouts  4.5 us
    ppermute x1, starting transfers between devices, shards(): back = lax.ppermute(back, 'space', one_on)  3.45 us
    all_to_all x1, starting transfers between devices, shards(): lax.all_to_all(pieces, 'bead', split_axis=0, concat_axis=0, tiled=True)  3.42 us
  transfers between devices with their start and end apart: 5, of which 3 were waited for; matrix products, arithmetic and copies ran while one was open for 1% of the time, Pallas kernels for 20%

commit v1 on v0

--- a/solution.py
+++ b/solution.py
@@ -22,7 +22,9 @@
 BF16 = jnp.bfloat16
 SPAN = 32
 GROUP = 4
-STEPS = ((SPAN // 2, 4), (SPAN // 2, 2), (SPAN // 2, 1), (SPAN, 2), (SPAN, 1))
+STEPS = ((24, 4), (24, 2), (24, 1), (40, 2), (40, 1), (32, 2), (32, 1))
+RUN_ROWS = {1: 24, 2: 40}
+SPARE = 40
 VMEM_LIMIT = 48 * 1024 * 1024
 
 
@@ -127,20 +129,23 @@
     lanes_ref, sizes_ref, rows_ref, size_ref, total_ref, back_ref = refs
     beads, lanes = lanes_ref.shape[0], lanes_ref.shape[-1]
     here = pl.ds(first, SPAN)
-    row_half, row_root = size_ref[cell, 0, here, :], size_ref[cell, 1, here, :]
+    tall = (SPAN // 8, 8, lanes)
+    row_half = size_ref[cell, 0, here, :].reshape(tall)
+    row_root = size_ref[cell, 1, here, :].reshape(tall)
     known = []
     for partner, _, _ in partners:
-        half = row_half + sizes_ref[partner, 0:1, :]
+        half = row_half + sizes_ref[partner, 0]
         s2 = half * half
         terms = (s2, CUBE_ROOT_TWO * s2, None if longer else 0.75 + 3.0 * s2)
-        known.append((s2, terms, row_root * sizes_ref[partner, 1:2, :]))
+        known.append((s2, terms, row_root * sizes_ref[partner, 1]))
     for bead in range(beads):
-        rows = [rows_ref[cell, bead, axis, here, :] for axis in range(3)]
+        rows = [rows_ref[cell, bead, axis, here, :].reshape(tall) for axis in range(3)]
         back = [None, None, None]
         for (partner, step_y, step_z), (s2, terms, depth) in zip(partners, known):
-            place = lanes_ref[bead, partner]
             apart = [
-                place[0:1] - rows[0], (place[1:2] + step_y) - rows[1], (place[2:3] + step_z) - rows[2]
+                lanes_ref[bead, partner, 0] - rows[0],
+                (lanes_ref[bead, partner, 1] + step_y) - rows[1],
+                (lanes_ref[bead, partner, 2] + step_z) - rows[2],
             ]
             radius_sq = apart[0] * apart[0] + apart[1] * apart[1] + apart[2] * apart[2]
             weight = depth * pair_weight(radius_sq + s2, radius_sq, terms, longer)
@@ -148,14 +153,32 @@
                 push = weight * apart[axis]
                 back[axis] = push if back[axis] is None else back[axis] + push
                 if total_ref is not None:
-                    total_ref[partner, bead, axis] += jnp.sum(
-                        push.reshape(SPAN // 8, 8, lanes), axis=0
-                    )
+                    total_ref[partner, bead, axis] += jnp.sum(push, axis=0)
         for axis in range(3):
+            value = back[axis].reshape(SPAN, lanes)
             if total_ref is None:
-                back_ref[cell, bead, axis, here, :] = back[axis]
+                back_ref[cell, bead, axis, here, :] = value
             else:
-                back_ref[cell, bead, axis, here, :] += back[axis]
+                back_ref[cell, bead, axis, here, :] += value
+
+
+def repeat_lanes(position, params, next_position, next_params, lanes_ref, sizes_ref):
+    beads, cells, _, lanes = position.shape
+
+    def per_cell(cell, carry):
+        for layer, place, values in ((0, position, params), (1, next_position, next_params)):
+            for kind in range(2):
+                sizes_ref[layer * cells + cell, kind] = jnp.broadcast_to(
+                    values[cell, kind : kind + 1, :], (8, lanes)
+                )
+            for bead in range(beads):
+                for axis in range(3):
+                    row = place[bead, cell, axis : axis + 1, :]
+                    row = row + 1.0 if layer == 1 and axis == 0 else row
+                    lanes_ref[bead, layer * cells + cell, axis] = jnp.broadcast_to(row, (8, lanes))
+        return carry
+
+    lax.fori_loop(0, cells, per_cell, 0)
 
 
 def fold_back(back_ref, cell, bead):
@@ -181,13 +204,7 @@
     beads, cells, _, lanes = position.shape
     factor = weight_factor(longer)
     together = max(1, 4 // beads)
-    axis_row = lax.broadcasted_iota(jnp.int32, (3, lanes), 0)
-    layer = jnp.where(axis_row == 0, 1.0, 0.0)
-    for bead in range(beads):
-        lanes_ref[bead, 0:cells] = position[bead]
-        lanes_ref[bead, cells : 2 * cells] = next_position[bead] + layer[None]
-    sizes_ref[0:cells] = params[:, 0:2, :]
-    sizes_ref[cells : 2 * cells] = next_params[:, 0:2, :]
+    repeat_lanes(position, params, next_position, next_params, lanes_ref, sizes_ref)
     total_ref[...] = jnp.zeros_like(total_ref)
 
     def spread(index, carry):
@@ -279,7 +296,7 @@
                 runs.setdefault(entry[4] - entry[3], []).append(entry)
         for length, entries in sorted(runs.items()):
             entries.sort(key=lambda entry: entry[3:])
-            span = SPAN // 2 if length == 1 else SPAN
+            span = RUN_ROWS.get(length, SPAN)
             for place, (rows, count) in enumerate(STEPS):
                 if rows == span:
                     whole = len(entries) // count * count
@@ -346,27 +363,29 @@
     for bead in range(beads):
         for firsts, partner, step_y, step_z in runs:
             here = pl.ds(firsts[bead], span)
-            half = rows_ref[local, bead, 3, here, :] + sizes_ref[partner, 0:1, :]
+            rows = [
+                rows_ref[local, bead, kind, here, :].reshape(span // 8, 8, lanes)
+                for kind in range(5)
+            ]
+            half = rows[3] + sizes_ref[partner, 0]
             s2 = half * half
             terms = (s2, CUBE_ROOT_TWO * s2, 0.75 + 3.0 * s2)
-            place = lanes_ref[bead, partner]
             apart = [
-                place[0:1] - rows_ref[local, bead, 0, here, :],
-                (place[1:2] + step_y) - rows_ref[local, bead, 1, here, :],
-                (place[2:3] + step_z) - rows_ref[local, bead, 2, here, :],
+                lanes_ref[bead, partner, 0] - rows[0],
+                (lanes_ref[bead, partner, 1] + step_y) - rows[1],
+                (lanes_ref[bead, partner, 2] + step_z) - rows[2],
             ]
             radius_sq = apart[0] * apart[0] + apart[1] * apart[1] + apart[2] * apart[2]
-            depth = rows_ref[local, bead, 4, here, :] * sizes_ref[partner, 1:2, :]
+            depth = rows[4] * sizes_ref[partner, 1]
             weight = depth * pair_weight(radius_sq + s2, radius_sq, terms, False)
             for axis in range(3):
                 push = weight * apart[axis]
+                flat_push = push.reshape(span, lanes)
                 if total_ref is None:
-                    back_ref[local, bead, axis, here, :] = push
+                    back_ref[local, bead, axis, here, :] = flat_push
                 else:
-                    back_ref[local, bead, axis, here, :] += push
-                    total_ref[partner, bead, axis] += jnp.sum(
-                        push.reshape(span // 8, 8, lanes), axis=0
-                    )
+                    back_ref[local, bead, axis, here, :] += flat_push
+                    total_ref[partner, bead, axis] += jnp.sum(push, axis=0)
 
 
 def reach_kernel(
@@ -377,15 +396,9 @@
     entries_at = len(STEPS) * (cells + 1)
     bounds_at = plan.shape[0] - beads * cells * 9
     factor = weight_factor(False)
-    axis_row = lax.broadcasted_iota(jnp.int32, (3, lanes), 0)
-    layer = jnp.where(axis_row == 0, 1.0, 0.0)
-    for bead in range(beads):
-        lanes_ref[bead, 0:cells] = position[bead]
-        lanes_ref[bead, cells : 2 * cells] = next_position[bead] + layer[None]
-    sizes_ref[0:cells] = params[:, 0:2, :]
-    sizes_ref[cells : 2 * cells] = next_params[:, 0:2, :]
+    repeat_lanes(position, params, next_position, next_params, lanes_ref, sizes_ref)
     total_ref[...] = jnp.zeros_like(total_ref)
-    rows_ref[:, :, :, lanes:, :] = jnp.zeros((GROUP, beads, 5, SPAN, lanes), F32)
+    rows_ref[:, :, :, lanes:, :] = jnp.zeros((GROUP, beads, 5, SPARE, lanes), F32)
     row = lax.broadcasted_iota(jnp.int32, (lanes, lanes), 0).astype(F32)
     slot = lax.broadcasted_iota(jnp.int32, (8, lanes), 1)
     column = lax.broadcasted_iota(jnp.int32, (lanes, 8), 1)
@@ -422,7 +435,9 @@
                     runs, longest = [], 0
                     for shift in range(count):
                         at = entries_at + 5 * (begin + step * count + shift)
-                        begins = [bound(bead, plan[at + 3]) for bead in range(beads)]
+                        begins = [
+                            lax.bitwise_and(bound(bead, plan[at + 3]), -8) for bead in range(beads)
+                        ]
                         for bead in range(beads):
                             longest = jnp.maximum(longest, bound(bead, plan[at + 4]) - begins[bead])
                         runs.append(
@@ -431,7 +446,13 @@
 
                     def per_span(index, carry):
                         moved = [
-                            ([jnp.minimum(first + index * span, lanes) for first in begins], *rest)
+                            (
+                                [
+                                    pl.multiple_of(jnp.minimum(first + index * span, lanes), 8)
+                                    for first in begins
+                                ],
+                                *rest,
+                            )
                             for begins, *rest in runs
                         ]
                         meet_runs(span, local, moved, *refs, total_ref, back_ref)
@@ -491,11 +512,11 @@
         1,
         (forces, forces),
         [
-            pltpu.VMEM((beads, 2 * cells, 3, lanes), F32),
-            pltpu.VMEM((2 * cells, 2, lanes), F32),
-            pltpu.VMEM((GROUP, beads, 5, lanes + SPAN, lanes), F32),
+            pltpu.VMEM((beads, 2 * cells, 3, 8, lanes), F32),
+            pltpu.VMEM((2 * cells, 2, 8, lanes), F32),
+            pltpu.VMEM((GROUP, beads, 5, lanes + SPARE, lanes), F32),
             pltpu.VMEM((2 * cells, beads, 3, 8, lanes), F32),
-            pltpu.VMEM((GROUP, beads, 3, lanes + SPAN, lanes), F32),
+            pltpu.VMEM((GROUP, beads, 3, lanes + SPARE, lanes), F32),
         ],
         PAIR_FLOPS * beads * 70,
     )
@@ -531,8 +552,8 @@
         2,
         (forces, forces),
         [
-            pltpu.VMEM((beads, 2 * cells, 3, lanes), F32),
-            pltpu.VMEM((2 * cells, 2, lanes), F32),
+            pltpu.VMEM((beads, 2 * cells, 3, 8, lanes), F32),
+            pltpu.VMEM((2 * cells, 2, 8, lanes), F32),
             pltpu.VMEM((cells, beads, 3, lanes, lanes), F32),
             pltpu.VMEM((cells, 2, lanes, lanes), F32),
             pltpu.VMEM((2 * cells, beads, 3, 8, lanes), F32),

time: 132 us -> 133 us (level); the launches traced: 134 us -> 131 us
  starting transfers between devices: 11.8 us -> 7.27 us
  blocking collectives: 34.8 us -> 30.6 us
  waiting for transfers between devices: 3.39 us -> 7.13 us
  Pallas kernels: 75.4 us -> 77.4 us
    ppermute x1, starting transfers between devices: 3.45 us -> 0.58 us  [shards(): back = lax.ppermute(back, 'space', one_on)]
    all_to_all x1, blocking collectives: 16.6 us -> 13.8 us  [shards(): lax.all_to_all(partial.reshape(holders, held * rows, lanes), 'bead', spli...]
    ppermute x1, waiting for transfers between devices: 0.86 us -> 2.92 us  [shards(): back = lax.ppermute(back, 'space', one_on)]
    pallas_call x6, Pallas kernels: 75.4 us -> 77.4 us  [call(): pl.pallas_call(kernel, out_shape=outputs, in_specs=[pl.BlockSpec(memory_s...]
    ppermute x1, waiting for transfers between devices: 0.94 us -> 2.61 us  [shards(): slow = slow + lax.ppermute(slow_back, 'space', one_on)]
    ppermute x1, starting transfers between devices: 2.43 us -> 0.75 us  [shards(): slow = slow + lax.ppermute(slow_back, 'space', one_on)]
  transfers between devices with their start and end apart: 5 -> 5, of which waited for: 3 -> 3; matrix products, arithmetic and copies ran while one was open for 1% -> 1% of each run, Pallas kernels for 20% -> 21%
where the time goes in v1:
time: 133 us; the launch traced here: 131 us
  Pallas kernels  77.4 us (58%)
  blocking collectives  30.6 us (23%)
  starting transfers between devices  7.27 us (5%)
  waiting for transfers between devices  7.13 us (5%)
  local copies, waits for them, and re-layouts  6.23 us (5%)
  other arithmetic  1.76 us (1%)
    pallas_call x6, Pallas kernels, call(): pl.pallas_call(kernel, out_shape=outputs, in_specs=[pl.BlockSpec(memory_s...  77.4 us
    all_to_all x1, blocking collectives, shards(): got = lax.all_to_all(sent, 'bead', split_axis=0, concat_axis=0, tiled=True)  16.8 us
    all_to_all x1, blocking collectives, shards(): lax.all_to_all(partial.reshape(holders, held * rows, lanes), 'bead', spli...  13.8 us
    unnamed x23, local copies, waits for them, and re-layouts  4.5 us
    all_to_all x1, starting transfers between devices, shards(): lax.all_to_all(pieces, 'bead', split_axis=0, concat_axis=0, tiled=True)  3.42 us
    ppermute x1, waiting for transfers between devices, shards(): back = lax.ppermute(back, 'space', one_on)  2.92 us
  transfers between devices with their start and end apart: 5, of which 3 were waited for; matrix products, arithmetic and copies ran while one was open for 1% of the time, Pallas kernels for 21%

profile of v1, /device:TPU:0, one launch (start us, length us, event | category | flops | bytes accessed | tf_op | source)
XLA Modules:
  0.0 131.2 jit_solution(10060645586297324030)
XLA Ops:
  0.6 0.8 select_reduce_fusion.2
  1.4 0.9 copy.36.position
  2.4 0.0 copy-start.3
  2.4 0.6 copy-done.3
  3.1 0.1 compare_select_fusion
  3.2 0.0 copy-start.5
  3.2 2.5 %collective-permute-start = (f32[5,16,3,128]{3,2,1,0:T(4,128)S(1)}, f32[5,16,3,128]{3,2,1,0:T(4,128)S(1)}, u32[]{:S(2)}, u32[]{:S(2)}) collective-permute-start(f32[5,16,3,128]{3,2,1,0:T(4,128)S(1)} %pad_maximum_fusion.1), channel_id=1, source_target_pairs={{1,0},{2,1},{3,2},{0,3},{5,4},{6,5},{7,6},{4,7},{9,8},{10,9},{11,1... | collective-permute-start | bytes 368648 | tf_op jit(solution)/shard_map/ppermute | solution.py:681
  5.7 0.1 iota_compare_fusion.2
  5.8 0.0 copy-done.5
  5.8 0.7 convert_reduce_fusion
  6.5 0.1 copy.32
  6.6 0.0 copy-start.8
  6.6 0.0 copy-start.9
  6.6 0.1 reshape.80
  6.7 0.5 copy-done.8
  7.3 0.0 copy-done.9
  7.3 0.1 concatenate.9.plan
  7.4 6.1 %shard_map.149.ordered = f32[4,16,8,128]{3,2,1,0:T(8,128)S(1)} custom-call(f32[4,16,3,128]{3,2,1,0:T(4,128)S(1)} %copy.36.position, f32[16,3,128]{2,1,0:T(4,128)S(1)} %get-tuple-element.26.params), custom_call_target="tpu_custom_call" | custom-call | flops 4194304 | bytes 262144 | tf_op jit(solution)/shard_map/pallas_call | solution.py:526
  13.5 0.0 collective-permute-done
  13.5 0.0 copy-start.6
  13.5 46.2 %shard_map.150 = (f32[4,16,3,128]{3,2,1,0:T(4,128)S(1)}, f32[4,16,3,128]{3,2,1,0:T(4,128)S(1)}) custom-call(s32[1405]{0:T(1024)S(1)} %concatenate.9.plan, f32[4,16,3,128]{3,2,1,0:T(4,128)S(1)} %copy.36.position, f32[16,3,128]{2,1,0:T(4,128)S(1)} %get-tuple-element.26.params, f32[4,16,3,128]{3,2,1,0:T(4,128)S(1)} %slice.28.next_position, ...), custom_call_target="tpu_custom_call" | custom-call | flops 183500800 | bytes 262144 | tf_op jit(solution)/shard_map/pallas_call | solution.py:526
  59.8 0.6 collective-permute-start.1
  60.3 0.0 copy-done.6
  60.3 0.0 copy-start.7
  60.3 0.1 copy.37.momenta
  60.4 0.8 copy-done.7
  61.2 0.0 copy-start.2
  61.2 0.1 copy.38.noise
  61.3 2.9 %collective-permute-done.1.back = f32[4,16,3,128]{3,2,1,0:T(4,128)S(1)} collective-permute-done((f32[4,16,3,128]{3,2,1,0:T(4,128)S(1)}, f32[4,16,3,128]{3,2,1,0:T(4,128)S(1)}, u32[]{:S(2)}, u32[]{:S(2)}) %collective-permute-start.1) | collective-permute-done | bytes 98336 | tf_op jit(solution)/shard_map/ppermute | solution.py:698
  64.2 0.0 copy-done.2
  64.2 2.6 %shard_map.151 = (f32[8,48,128]{2,1,0:T(8,128)S(1)}, f32[8,72,128]{2,1,0:T(8,128)}) custom-call(f32[8,96]{1,0:T(8,128)S(1)} %copy-done.2, s32[1]{0:T(128)} %bitcast.rank, f32[4,16,3,128]{3,2,1,0:T(4,128)S(1)} %copy.36.position, f32[4,16,3,128]{3,2,1,0:T(4,128)S(1)} %copy.37.momenta, f32[4,16,3,128]{3,2,1,0:T(4,128)S(1)} %copy.38.noise, ...), custom_call_target="tpu_custom_call" | custom-call | flops 4194304 | bytes 262144 | tf_op jit(solution)/shard_map/pallas_call | solution.py:526
  66.8 13.8 %all_to_all.15 = f32[8,48,128]{2,1,0:T(8,128)S(1)} all-to-all(f32[8,48,128]{2,1,0:T(8,128)S(1)} %get-tuple-element.11), channel_id=1, replica_groups=mesh['bead'=8,'space'=4] {'bead'}, dimensions={0} | all-to-all | bytes 393216 | tf_op jit(solution)/shard_map/all_to_all | solution.py:715
  80.6 3.4 %all-to-all-start = ((f32[8,72,128]{2,1,0:T(8,128)}), f32[8,72,128]{2,1,0:T(8,128)S(1)}, u32[]{:S(2)}, u32[]{:S(2)}) async-start(f32[8,72,128]{2,1,0:T(8,128)} %get-tuple-element.10), calls=%async_computation | async-start | bytes 589824 | tf_op jit(solution)/shard_map/all_to_all | solution.py:720
  84.0 0.0 copy-start.4
  84.1 0.1 collective-permute-start.2
  84.1 1.6 %collective-permute-done.2.next_position = f32[1,16,3,128]{3,2,1,0:T(4,128)S(1)} collective-permute-done((f32[1,16,3,128]{3,2,1,0:T(4,128)S(1)}, f32[1,16,3,128]{3,2,1,0:T(4,128)S(1)}, u32[]{:S(2)}, u32[]{:S(2)}) %collective-permute-start.2) | collective-permute-done | bytes 24608 | tf_op jit(solution)/shard_map/ppermute | solution.py:719
  85.7 0.0 copy-done.4
  85.7 21.1 %shard_map.153 = (f32[1,16,3,128]{3,2,1,0:T(4,128)S(1)}, f32[1,16,3,128]{3,2,1,0:T(4,128)S(1)}) custom-call(s32[443]{0:T(512)S(1)} %copy-done.4, s32[16]{0:T(128)S(1)} %copy-done.3, f32[1,16,3,128]{3,2,1,0:T(4,128)S(1)} %reshape.81.position, f32[16,3,128]{2,1,0:T(4,128)S(1)} %get-tuple-element.26.params, ...), custom_call_target="tpu_custom_call" | custom-call | flops 103546880 | bytes 262144 | tf_op jit(solution)/shard_map/pallas_call | solution.py:526
  106.8 0.8 collective-permute-start.3
  107.6 2.6 %collective-permute-done.3 = f32[1,16,3,128]{3,2,1,0:T(4,128)S(1)} collective-permute-done((f32[1,16,3,128]{3,2,1,0:T(4,128)S(1)}, f32[1,16,3,128]{3,2,1,0:T(4,128)S(1)}, u32[]{:S(2)}, u32[]{:S(2)}) %collective-permute-start.3) | collective-permute-done | bytes 24608 | tf_op jit(solution)/shard_map/ppermute | solution.py:724
  110.2 0.0 copy-start
  110.3 0.0 all-to-all-done.arrived
  110.3 0.7 copy-done
  111.0 0.4 shard_map.152
  111.4 16.8 %all_to_all.16 = f32[8,96,128]{2,1,0:T(8,128)S(1)} all-to-all(f32[8,96,128]{2,1,0:T(8,128)S(1)} %pad_maximum_fusion), channel_id=1, replica_groups=mesh['bead'=8,'space'=4] {'bead'}, dimensions={0} | all-to-all | bytes 786432 | tf_op jit(solution)/shard_map/all_to_all | solution.py:744
  128.3 0.0 copy-start.1
  128.3 0.7 copy-done.1
  128.9 1.0 shard_map.154
  129.9 0.6 copy.39
  130.6 0.6 copy.40
  (14 shorter events, 0.3 us)
Async XLA Ops:
  2.4 0.7 copy-start.3
  3.2 2.6 %copy-start.5 = (f32[4,16,3,128]{3,1,2,0:T(8,128)S(1)}, f32[4,16,3,128]{3,1,2,0:T(8,128)}, u32[]{:S(2)}) copy-start(f32[4,16,3,128]{3,1,2,0:T(8,128)} %param.14) | copy-start | bytes 294916
  3.2 10.2 %collective-permute-start = (f32[5,16,3,128]{3,2,1,0:T(4,128)S(1)}, f32[5,16,3,128]{3,2,1,0:T(4,128)S(1)}, u32[]{:S(2)}, u32[]{:S(2)}) collective-permute-start(f32[5,16,3,128]{3,2,1,0:T(4,128)S(1)} %pad_maximum_fusion.1), channel_id=1, source_target_pairs={{1,0},{2,1},{3,2},{0,3},{5,4},{6,5},{7,6},{4,7},{9,8},{10,9},{11,1... | collective-permute-start | bytes 368648 | tf_op jit(solution)/shard_map/ppermute | solution.py:681
  6.6 0.7 copy-start.8
  6.6 0.7 copy-start.9
  13.5 46.8 %copy-start.6 = (f32[4,16,3,128]{3,1,2,0:T(8,128)S(1)}, f32[4,16,3,128]{3,1,2,0:T(8,128)}, u32[]{:S(2)}) copy-start(f32[4,16,3,128]{3,1,2,0:T(8,128)} %param.15) | copy-start | bytes 294916
  59.8 4.4 %collective-permute-start.1 = (f32[4,16,3,128]{3,2,1,0:T(4,128)S(1)}, f32[4,16,3,128]{3,2,1,0:T(4,128)S(1)}, u32[]{:S(2)}, u32[]{:S(2)}) collective-permute-start(f32[4,16,3,128]{3,2,1,0:T(4,128)S(1)} %get-tuple-element.9), channel_id=1, source_target_pairs={{0,1},{1,2},{2,3},{3,0},{4,5},{5,6},{6,7},{7,4},{8,9},{9,10},{10,1... | collective-permute-start | bytes 294920 | tf_op jit(solution)/shard_map/ppermute | solution.py:698
  60.3 0.9 copy-start.7
  61.2 3.0 %copy-start.2 = (f32[8,96]{1,0:T(8,128)S(1)}, f32[8,96]{1,0:T(8,128)}, u32[]{:S(2)}) copy-start(f32[8,96]{1,0:T(8,128)} %constant.35.clone.table) | copy-start | bytes 9220
  80.6 29.7 %all-to-all-start = ((f32[8,72,128]{2,1,0:T(8,128)}), f32[8,72,128]{2,1,0:T(8,128)S(1)}, u32[]{:S(2)}, u32[]{:S(2)}) async-start(f32[8,72,128]{2,1,0:T(8,128)} %get-tuple-element.10), calls=%async_computation | async-start | bytes 589824 | tf_op jit(solution)/shard_map/all_to_all | solution.py:720
  84.0 1.7 %copy-start.4 = (s32[443]{0:T(512)S(1)}, s32[443]{0:T(512)}, u32[]{:S(2)}) copy-start(s32[443]{0:T(512)} %constant.36.clone.plan) | copy-start | bytes 5320
  84.1 1.7 %collective-permute-start.2 = (f32[1,16,3,128]{3,2,1,0:T(4,128)S(1)}, f32[1,16,3,128]{3,2,1,0:T(4,128)S(1)}, u32[]{:S(2)}, u32[]{:S(2)}) collective-permute-start(f32[1,16,3,128]{3,2,1,0:T(4,128)S(1)} %reshape.81.position), channel_id=1, source_target_pairs={{1,0},{2,1},{3,2},{0,3},{5,4},{6,5},{7,6},{4,7},{9,8},{10,9},{11,1... | collective-permute-start | bytes 73736 | tf_op jit(solution)/shard_map/ppermute | solution.py:719
  106.8 3.4 %collective-permute-start.3 = (f32[1,16,3,128]{3,2,1,0:T(4,128)S(1)}, f32[1,16,3,128]{3,2,1,0:T(4,128)S(1)}, u32[]{:S(2)}, u32[]{:S(2)}) collective-permute-start(f32[1,16,3,128]{3,2,1,0:T(4,128)S(1)} %get-tuple-element.13), channel_id=1, source_target_pairs={{0,1},{1,2},{2,3},{3,0},{4,5},{5,6},{6,7},{7,4},{8,9},{9,10},{10,1... | collective-permute-start | bytes 73736 | tf_op jit(solution)/shard_map/ppermute | solution.py:724
  110.2 0.8 copy-start
  128.3 0.7 copy-start.1
